TPU v7x, 32 devices: a whole 2x2x4 slice. The times are simulated.
32 devices in a mesh: groups: 2 (over y), dp: 4 (over z), mp: 2 (over x), sub: 2 (over core).
Axes of the slice: x: 2, y: 2, z: 4, core: 2. Of those that a mesh axis runs over, the one named last changes fastest.
Arguments:
- hidden: bfloat16 [4096, 14336], P(('groups', 'dp', 'sub'), 'mp'), parts along dimension 0, may hold values from -6 to 6
- out_grad: bfloat16 [4096, 4096], P(('groups', 'dp', 'sub'), 'mp'), parts along dimension 0, may hold values from -80 to 80
- lengths: int32 [64], P(('groups', 'dp', 'sub')), parts along dimension 0, may hold values from 16 to 64
- proj_in: bfloat16 [14336, 32], P('mp'), may hold values from -0.005859375 to 0.005859375
- proj_out: bfloat16 [4096, 32], P('mp'), may hold values from -0.09375 to 0.09375
- test_proj: bfloat16 [2048, 1024], P(('mp', 'sub')), may hold values from -6 to 6
Outputs:
- covariance: float32 [2048, 1024], P(('groups', 'dp', 'sub')), parts along dimension 0
- scores: float32 [64, 2048], P(('groups', 'dp', 'sub'), 'mp'), parts along dimension 0
There are 2 independent parts, one for each index of `groups`. A program takes and returns all parts, laid end to end along the dimension named above; an argument that names none is the same for every part. Nothing has to cross between parts.
All inputs are finite; a program needn't handle non-finite values.
Results may differ from a plain program's by a relative error of at most 0.004.
Values may be sent and summed in bfloat16 or wider, within the bound.
No kernel may reach another device: no remote copies, remote signals or barrier semaphores. Data moves between devices by JAX's collectives and lax.ppermute only.
A program may use at most 64 MiB of HBM per device.

v0:
```python
import jax
import jax.numpy as jnp
from jax import lax
from jax.sharding import PartitionSpec as P

SEQ = 64


def per_device(hidden, out_grad, lengths, proj_in, proj_out, test_proj):
    rows = hidden.shape[0]
    count = lengths.shape[0]
    width_in = proj_in.shape[1]
    width_out = proj_out.shape[1]
    flat = width_in * width_out
    slots = jnp.arange(rows, dtype=jnp.int32) % SEQ
    limits = jnp.repeat(lengths, SEQ, total_repeat_length=rows)
    mask = (slots < limits).astype(jnp.float32)
    part_in = jnp.dot(hidden, proj_in, preferred_element_type=jnp.float32)
    part_out = jnp.dot(out_grad, proj_out, preferred_element_type=jnp.float32)
    act_proj, grad_proj = lax.psum((part_in, part_out), "mp")
    act_proj = act_proj * mask[:, None]
    grads = jnp.einsum(
        "eti,etj->eij",
        act_proj.reshape(count, SEQ, width_in),
        grad_proj.reshape(count, SEQ, width_out),
        precision=lax.Precision.HIGHEST,
    )
    grads = grads.reshape(count, flat).astype(jnp.bfloat16)
    sharers = lax.axis_size(("dp", "sub"))
    examples_all = count * sharers
    partial_cov = jnp.einsum("ek,el->kl", grads, grads, preferred_element_type=jnp.float32)
    summed = lax.psum_scatter(partial_cov, ("dp", "sub"), scatter_dimension=0, tiled=True)
    wide = grads.astype(jnp.float32)
    total = lax.psum(jnp.sum(wide * wide), ("dp", "sub"))
    covariance = summed / examples_all
    factor = lax.rsqrt(total / examples_all + 1e-06)
    tests = lax.all_gather(test_proj, "sub", axis=0, tiled=True)
    scores = jnp.einsum("ep,qp->eq", grads, tests, preferred_element_type=jnp.float32) * factor
    return (covariance, scores)


def solution(mesh):
    in_specs = (
        P(("groups", "dp", "sub"), "mp"),
        P(("groups", "dp", "sub"), "mp"),
        P(("groups", "dp", "sub")),
        P("mp", None),
        P("mp", None),
        P(("mp", "sub"), None),
    )
    out_specs = (P(("groups", "dp", "sub"), None), P(("groups", "dp", "sub"), "mp"))
    return jax.shard_map(
        per_device, mesh=mesh, in_specs=in_specs, out_specs=out_specs, check_vma=False
    )
```

profile of v0, /device:TPU:0, one launch (start us, length us, event | category | flops | bytes accessed | tf_op | source)
XLA Modules:
  0.0 104.3 jit_solution(1899970995674611639)
XLA Ops:
  8.0 0.0 copy-start
  8.0 0.0 copy-start.2
  8.0 0.0 copy-start.1
  8.0 0.0 all-reduce.3.cloned.1.call-start
  8.1 1.2 %copy-done = bf16[256,2048]{1,0:T(8,128)(2,1)S(1)} copy-done((bf16[256,2048]{1,0:T(8,128)(2,1)S(1)}, bf16[256,2048]{1,0:T(8,128)(2,1)}, u32[]{:S(2)}) %copy-start) | copy-done | bytes 1048600
  9.2 1.3 %fusion.3 = f32[256,32]{0,1:T(8,128)S(1)} fusion(bf16[256,2048]{1,0:T(8,128)(2,1)S(1)} %copy-done, bf16[2048,32]{0,1:T(8,128)(2,1)} %param.12), kind=kOutput, calls=%fused_computation.19 | convolution fusion | flops 33554432 | bytes 1212416 | tf_op jit(solution)/shard_map/dot_general | solution.py:19
  10.6 0.1 reshape.116
  10.7 0.6 copy.8
  11.3 3.9 %fusion.2 = f32[256,32]{0,1:T(8,128)} fusion(bf16[256,7168]{1,0:T(8,128)(2,1)} %param.8, bf16[7168,32]{0,1:T(8,128)(2,1)} %param.11), kind=kOutput, calls=%fused_computation.18 | convolution fusion | flops 117440512 | bytes 4161536 | tf_op jit(solution)/shard_map/dot_general | solution.py:18
  15.2 0.0 all-reduce.3.cloned.1.call-update
  15.3 0.0 all-gather.2.cloned.1.call-start
  15.3 0.5 all-gather.2.cloned.1.call-update
  15.8 0.0 reduce-scatter.2.cloned.1.call-start
  15.9 0.0 copy-done.1
  15.9 0.6 fusion.1
  16.6 0.0 copy-done.2
  16.6 0.1 add_add_fusion.1
  16.6 2.5 %compare_select_fusion.1 = s32[256,1]{0,1:T(1,128)S(1)} fusion(s32[256,1]{0,1:T(1,128)S(1)} %bitcast.26, s32[256,1]{0,1:T(1,128)S(1)} %bitcast.25, s32[]{:T(128)} %bitcast.4, s32[]{:T(128)} %bitcast.5, s32[]{:T(128)} %bitcast.7, s32[]{:T(128)} %bitcast.6), kind=kLoop, calls=%fused_computation.7 | loop fusion | flops 2048 | bytes 3088 | tf_op jit(solution)/shard_map/jit(_take)/gather | solution.py:16
  19.1 0.1 compare_convert_fusion
  19.2 20.1 %all-reduce.3.cloned.1.call-done = (f32[4,64,32]{1,2,0:T(8,128)}, f32[256,32]{0,1:T(8,128)}) async-done(((f32[4,64,32]{1,2,0:T(8,128)}, f32[256,32]{0,1:T(8,128)}), (f32[4,64,32]{1,2,0:T(8,128)}, f32[256,32]{0,1:T(8,128)})) %all-reduce.3.cloned.1.call-update) | async-done | bytes 65552 | tf_op jit(solution)/shard_map/psum | solution.py:20
  39.3 0.8 broadcast_multiply_fusion.1
  40.0 0.1 reshape.115
  40.1 1.7 %multiply_reduce_fusion = (f32[]{:T(128)}, bf16[4,32,32]{2,1,0:T(8,128)(2,1)S(1)}) fusion(f32[4,64,32]{1,2,0:T(8,128)} %get-tuple-element.14, f32[4,64,32]{1,0,2:T(4,128)S(1)} %reshape.115), kind=kOutput, calls=%fused_computation.4 | convolution fusion | flops 3162111 | bytes 73732 | tf_op jit(solution)/shard_map/eti,etj->eij/dot_general | solution.py:22
  41.8 0.1 convert_element_type.22
  41.9 2.7 %fusion.4 = f32[1024,1024]{1,0:T(8,128)} fusion(bf16[4,1024]{1,0:T(4,128)(2,1)S(1)} %convert_element_type.22), kind=kOutput, calls=%fused_computation.20 | convolution fusion | flops 8388608 | bytes 4202496 | tf_op jit(solution)/shard_map/ek,el->kl/dot_general | solution.py:31
  44.6 0.0 reduce-scatter.2.cloned.1.call-update
  44.6 17.0 %psum.23 = f32[]{:T(128)} all-reduce(f32[]{:T(128)} %get-tuple-element.22), channel_id=1, replica_groups=mesh['groups'=2,'dp'=4,'mp'=2,'sub'=2] {'dp','sub'}, use_global_device_ids=true, to_apply=%region_4.5 | all-reduce | flops 1 | bytes 8 | tf_op jit(solution)/shard_map/psum | solution.py:34
  62.3 0.0 all-gather.2.cloned.1.call-done
  62.3 2.9 %convolution_multiply_fusion = f32[4,1024]{1,0:T(4,128)} fusion(bf16[4,1024]{1,0:T(4,128)(2,1)S(1)} %convert_element_type.22, bf16[1024,1024]{1,0:T(8,128)(2,1)} %all-gather.2.cloned.1.call-done, f32[]{:T(128)S(6)} %rsqrt.3), kind=kOutput, calls=%fused_computation.1 | convolution fusion | flops 8392704 | bytes 2121732 | tf_op jit(solution)/shard_map/ep,qp->eq/dot_general | solution.py:38
  65.2 29.7 %reduce-scatter.2.cloned.1.call-done = f32[128,1024]{1,0:T(8,128)} async-done(((f32[1024,1024]{1,0:T(8,128)}), f32[128,1024]{1,0:T(8,128)}) %reduce-scatter.2.cloned.1.call-update) | async-done | bytes 524304 | tf_op jit(solution)/shard_map/reduce_scatter | solution.py:32
  94.9 1.9 %broadcast_multiply_fusion = f32[128,1024]{1,0:T(8,128)} fusion(f32[128,1024]{1,0:T(8,128)} %reduce-scatter.2.cloned.1.call-done), kind=kLoop, calls=%fused_computation.2 | loop fusion | flops 131072 | bytes 1048576 | tf_op jit(solution)/shard_map/div | solution.py:35
  (1 shorter events, 0.0 us)
Async XLA Ops:
  8.0 1.2 %copy-start = (bf16[256,2048]{1,0:T(8,128)(2,1)S(1)}, bf16[256,2048]{1,0:T(8,128)(2,1)}, u32[]{:S(2)}) copy-start(bf16[256,2048]{1,0:T(8,128)(2,1)} %param.9) | copy-start | bytes 3145732
  8.0 8.5 %copy-start.2 = (s32[2,128]{1,0:T(2,128)S(1)}, s32[2,128]{1,0:T(2,128)}, u32[]{:S(2)}) copy-start(s32[2,128]{1,0:T(2,128)} %constant.105.clone.1) | copy-start | bytes 3076
  8.0 7.9 %copy-start.1 = (s32[4]{0:T(128)S(1)}, s32[4]{0:T(128)}, u32[]{:S(2)}) copy-start(s32[4]{0:T(128)} %param.10) | copy-start | bytes 52
  8.0 31.2 %all-reduce.3.cloned.1.call-start = ((), (), s32[]{:S(2)}) async-start(), calls=%async_computation.3 | async-start | bytes 196608 | tf_op jit(solution)/shard_map/psum | solution.py:20
  15.3 47.0 %all-gather.2.cloned.1.call-start = ((), (), s32[]{:S(2)}) async-start(), calls=%async_computation.2 | async-start | bytes 3145728 | tf_op jit(solution)/shard_map/all_gather | solution.py:37
  15.8 79.1 %reduce-scatter.2.cloned.1.call-start = ((), (), s32[]{:S(2)}) async-start(), calls=%async_computation.1 | async-start | bytes 4718592 | tf_op jit(solution)/shard_map/reduce_scatter | solution.py:32
Sparse Core Ops, SparseCore 0:
  15.4 23.8 all-reduce.2
  44.8 50.1 reduce-scatter.1
Sparse Core Ops, SparseCore 1:
  17.3 13.1 all-gather.1
where the time goes:
time: 105 us; the launch traced here: 104 us
  waiting for transfers between devices  50.4 us (48%)
  blocking collectives  17 us (16%)
  between operations  16.3 us (16%)
  matrix products  12.5 us (12%)
  other arithmetic  5.25 us (5%)
  local copies, waits for them, and re-layouts  2.75 us (3%)
    reduce_scatter x1, waiting for transfers between devices, per_device(): lax.psum_scatter(partial_cov, ('dp', 'sub'), scatter_dimension=0, tiled=T...  29.7 us
    psum x1, waiting for transfers between devices, per_device(): act_proj, grad_proj = lax.psum((part_in, part_out), 'mp')  20.1 us
    psum x1, blocking collectives, per_device(): total = lax.psum(jnp.sum(wide * wide), ('dp', 'sub'))  17 us
    dot_general x1, matrix products, per_device(): part_in = jnp.dot(hidden, proj_in, preferred_element_type=jnp.float32)  3.93 us
    dot_general x1, matrix products, per_device(): jnp.einsum('ep,qp->eq', grads, tests, preferred_element_type=jnp.float32)  2.88 us
    dot_general x1, matrix products, per_device(): jnp.einsum('ek,el->kl', grads, grads, preferred_element_type=jnp.float32)  2.69 us
    gather x1, other arithmetic, per_device(): limits = jnp.repeat(lengths, SEQ, total_repeat_length=rows)  2.46 us
  transfers between devices with their start and end apart: 3, of which 2 were waited for; matrix products, arithmetic and copies ran while one was open for 11% of the time, Pallas kernels for 0%

commit v1 on v0

v1 whole, which is shorter than its diff:
```python
import jax
import jax.numpy as jnp
from jax import lax
from jax.sharding import PartitionSpec as P

SEQ = 64


def gather_all(block, axes):
    n = lax.axis_size(axes)
    if n > 8:
        return lax.all_gather(block, axes)
    me = lax.axis_index(axes)
    got = [block]
    for step in range(1, n):
        got.append(lax.ppermute(block, axes, [(i, (i + step) % n) for i in range(n)]))
    stacked = jnp.stack(got)
    order = (me - jnp.arange(n)) % n
    return jnp.take(stacked, order, axis=0, mode="clip")


def sum_over(part, axis):
    n = lax.axis_size(axis)
    if n == 2:
        return part + lax.ppermute(part, axis, [(0, 1), (1, 0)])
    return lax.psum(part, axis)


def per_device(hidden, out_grad, lengths, proj_in, proj_out, test_proj):
    rows = hidden.shape[0]
    count = lengths.shape[0]
    width_in = proj_in.shape[1]
    width_out = proj_out.shape[1]
    flat = width_in * width_out
    sharers = lax.axis_size(("dp", "sub"))
    examples_all = count * sharers
    n_sub = lax.axis_size("sub")
    mask = (jnp.arange(SEQ, dtype=jnp.int32)[None, :] < lengths[:, None]).astype(jnp.float32)

    if n_sub == 2:
        other = lax.ppermute(test_proj, "sub", [(0, 1), (1, 0)])
    part_in = jnp.dot(hidden, proj_in, preferred_element_type=jnp.float32)
    part_out = jnp.dot(out_grad, proj_out, preferred_element_type=jnp.float32)
    both = sum_over(jnp.concatenate([part_in, part_out], axis=1), "mp")
    both = both.reshape(count, SEQ, width_in + width_out)
    act_proj = both[:, :, :width_in] * mask[:, :, None]
    grad_proj = both[:, :, width_in:]
    grads = jnp.einsum("eti,etj->eij", act_proj, grad_proj, precision=lax.Precision.HIGHEST)
    grads = grads.reshape(count, flat).astype(jnp.bfloat16)

    every = gather_all(grads, ("dp", "sub")).reshape(examples_all, flat)
    own_rows = flat // sharers
    mine = lax.dynamic_slice_in_dim(every, lax.axis_index(("dp", "sub")) * own_rows, own_rows, axis=1)
    covariance = jnp.einsum("ek,el->kl", mine, every, preferred_element_type=jnp.float32) / examples_all
    wide = every.astype(jnp.float32)
    total = jnp.sum(wide * wide)
    factor = lax.rsqrt(total / examples_all + 1e-06)
    if n_sub == 2:
        near = jnp.einsum("ep,qp->eq", grads, test_proj, preferred_element_type=jnp.float32)
        far = jnp.einsum("ep,qp->eq", grads, other, preferred_element_type=jnp.float32)
        first = lax.axis_index("sub") == 0
        scores = jnp.concatenate([jnp.where(first, near, far), jnp.where(first, far, near)], axis=1)
    else:
        tests = lax.all_gather(test_proj, "sub", axis=0, tiled=True)
        scores = jnp.einsum("ep,qp->eq", grads, tests, preferred_element_type=jnp.float32)
    return (covariance, scores * factor)


def solution(mesh):
    in_specs = (
        P(("groups", "dp", "sub"), "mp"),
        P(("groups", "dp", "sub"), "mp"),
        P(("groups", "dp", "sub")),
        P("mp", None),
        P("mp", None),
        P(("mp", "sub"), None),
    )
    out_specs = (P(("groups", "dp", "sub"), None), P(("groups", "dp", "sub"), "mp"))
    return jax.shard_map(
        per_device, mesh=mesh, in_specs=in_specs, out_specs=out_specs, check_vma=False
    )
```

time: 105 us -> 28.8 us (0.27)
  waiting for transfers between devices: 50.4 us -> 3.45 us
  blocking collectives: 17 us -> 0 us
  between operations: 16.3 us -> 1.49 us
  starting transfers between devices: 0.12 us -> 13.1 us
  matrix products: 12.5 us -> 6.66 us
  other arithmetic: 5.25 us -> 1.4 us
    reduce_scatter x1 -> x0, waiting for transfers between devices: 29.7 us -> none  [per_device(): lax.psum_scatter(partial_cov, ('dp', 'sub'), scatter_dimension=0, tiled=T...]
    psum x1 -> x0, waiting for transfers between devices: 20.1 us -> none  [per_device(): act_proj, grad_proj = lax.psum((part_in, part_out), 'mp')]
    psum x1 -> x0, blocking collectives: 17 us -> none  [per_device(): total = lax.psum(jnp.sum(wide * wide), ('dp', 'sub'))]
    ppermute x0 -> x9, starting transfers between devices: none -> 13.1 us  [the longest x7 10.1 us: gather_all(): lax.ppermute(block, axes, [(i, (i + step) % n) for i in range(n)])]
    dot_general x3 -> x4, matrix products: 7.25 us -> 2.02 us  [the longest x1 1.05 us: per_device(): jnp.einsum('ek,el->kl', mine, every, preferred_element_type=jnp.float32)]
    ppermute x0 -> x9, waiting for transfers between devices: none -> 3.45 us  [the longest x1 2.13 us: sum_over(): return part + lax.ppermute(part, axis, [(0, 1), (1, 0)])]
    gather x1, other arithmetic: 2.46 us -> 0.01 us  [gather_all(): return jnp.take(stacked, order, axis=0, mode='clip')]
    div x1 -> x0, other arithmetic: 1.88 us -> none  [per_device(): covariance = summed / examples_all]
  transfers between devices with their start and end apart: 3 -> 9, of which waited for: 2 -> 3; matrix products, arithmetic and copies ran while one was open for 11% -> 12% of each run, Pallas kernels for 0% -> 0%
where the time goes in v1:
time: 28.8 us; the launch traced here: 28.3 us
  starting transfers between devices  13.1 us (45%)
  matrix products  6.66 us (23%)
  waiting for transfers between devices  3.45 us (12%)
  local copies, waits for them, and re-layouts  2.27 us (8%)
  between operations  1.49 us (5%)
  other arithmetic  1.4 us (5%)
    ppermute x7, starting transfers between devices, gather_all(): lax.ppermute(block, axes, [(i, (i + step) % n) for i in range(n)])  10.1 us
    dot_general x1, matrix products, per_device(): part_in = jnp.dot(hidden, proj_in, preferred_element_type=jnp.float32)  3.31 us
    ppermute x1, starting transfers between devices, sum_over(): return part + lax.ppermute(part, axis, [(0, 1), (1, 0)])  3 us
    ppermute x1, waiting for transfers between devices, sum_over(): return part + lax.ppermute(part, axis, [(0, 1), (1, 0)])  2.13 us
    dot_general x1, matrix products, per_device(): part_out = jnp.dot(out_grad, proj_out, preferred_element_type=jnp.float32)  1.32 us
    ppermute x7, waiting for transfers between devices, gather_all(): lax.ppermute(block, axes, [(i, (i + step) % n) for i in range(n)])  1.31 us
    unnamed x13, local copies, waits for them, and re-layouts  1.3 us
    dot_general x1, matrix products, per_device(): jnp.einsum('ek,el->kl', mine, every, preferred_element_type=jnp.float32)  1.05 us
  transfers between devices with their start and end apart: 9, of which 3 were waited for; matrix products, arithmetic and copies ran while one was open for 12% of the time, Pallas kernels for 0%

profile of v1, /device:TPU:0, one launch (start us, length us, event | category | flops | bytes accessed | tf_op | source)
XLA Modules:
  0.0 28.3 jit_solution(16683249275617814077)
XLA Ops:
  0.6 0.0 copy-start
  0.7 1.2 %copy-done = bf16[256,2048]{1,0:T(8,128)(2,1)S(1)} copy-done((bf16[256,2048]{1,0:T(8,128)(2,1)S(1)}, bf16[256,2048]{1,0:T(8,128)(2,1)}, u32[]{:S(2)}) %copy-start) | copy-done | bytes 1048600
  1.9 1.3 %fusion.10 = f32[256,32]{0,1:T(8,128)S(1)} fusion(bf16[256,2048]{1,0:T(8,128)(2,1)S(1)} %copy-done, bf16[2048,32]{0,1:T(8,128)(2,1)} %param.10), kind=kOutput, calls=%fused_computation.32 | convolution fusion | flops 33554432 | bytes 1212416 | tf_op jit(solution)/shard_map/dot_general | solution.py:43
  3.2 3.3 %fusion.9 = f32[256,32]{0,1:T(8,128)S(1)} fusion(bf16[256,7168]{1,0:T(8,128)(2,1)} %param.6, bf16[7168,32]{0,1:T(8,128)(2,1)} %param.9), kind=kOutput, calls=%fused_computation.31 | convolution fusion | flops 117440512 | bytes 4161536 | tf_op jit(solution)/shard_map/dot_general | solution.py:42
  6.5 3.0 %collective-permute-start = (f32[256,64]{0,1:T(8,128)S(1)}, f32[256,64]{0,1:T(8,128)S(1)}, u32[]{:S(2)}, u32[]{:S(2)}) collective-permute-start(f32[256,64]{0,1:T(8,128)S(1)} %pad_maximum_fusion), channel_id=1, source_target_pairs={{0,2},{2,0},{1,3},{3,1},{4,6},{6,4},{5,7},{7,5},{8,10},{10,8},{9,1... | collective-permute-start | bytes 196616 | tf_op jit(solution)/shard_map/ppermute | solution.py:25
  9.6 0.0 collective-permute-start.8
  9.6 0.1 fusion.3
  9.7 2.1 %collective-permute-done = f32[256,64]{0,1:T(8,128)S(1)} collective-permute-done((f32[256,64]{0,1:T(8,128)S(1)}, f32[256,64]{0,1:T(8,128)S(1)}, u32[]{:S(2)}, u32[]{:S(2)}) %collective-permute-start) | collective-permute-done | bytes 65568 | tf_op jit(solution)/shard_map/ppermute | solution.py:25
  11.8 0.1 reshape.85
  11.9 0.2 convolution_convert_fusion
  12.2 0.1 convert_element_type.30
  12.3 0.1 convert_element_type.29
  12.4 0.1 collective-permute-start.1
  12.4 2.2 %collective-permute-start.2 = (bf16[4,1024]{1,0:T(4,128)(2,1)S(1)}, bf16[4,1024]{1,0:T(4,128)(2,1)S(1)}, u32[]{:S(2)}, u32[]{:S(2)}) collective-permute-start(bf16[4,1024]{1,0:T(4,128)(2,1)S(1)} %convert_element_type.30), channel_id=1, source_target_pairs={{0,4},{1,5},{4,8},{5,9},{8,12},{9,13},{12,0},{13,1},{2,6},{3,7},{6... | collective-permute-start | bytes 24584 | tf_op jit(solution)/shard_map/ppermute | solution.py:16
  14.6 2.5 %collective-permute-start.3 = (bf16[4,1024]{1,0:T(4,128)(2,1)S(1)}, bf16[4,1024]{1,0:T(4,128)(2,1)S(1)}, u32[]{:S(2)}, u32[]{:S(2)}) collective-permute-start(bf16[4,1024]{1,0:T(4,128)(2,1)S(1)} %convert_element_type.30), channel_id=1, source_target_pairs={{0,5},{1,8},{4,9},{5,12},{8,13},{9,0},{12,1},{13,4},{2,7},{3,10},{... | collective-permute-start | bytes 24584 | tf_op jit(solution)/shard_map/ppermute | solution.py:16
  17.1 1.2 %collective-permute-start.4 = (bf16[4,1024]{1,0:T(4,128)(2,1)S(1)}, bf16[4,1024]{1,0:T(4,128)(2,1)S(1)}, u32[]{:S(2)}, u32[]{:S(2)}) collective-permute-start(bf16[4,1024]{1,0:T(4,128)(2,1)S(1)} %convert_element_type.30), channel_id=1, source_target_pairs={{0,8},{1,9},{4,12},{5,13},{8,0},{9,1},{12,4},{13,5},{2,10},{3,11},... | collective-permute-start | bytes 24584 | tf_op jit(solution)/shard_map/ppermute | solution.py:16
  18.4 0.4 %fusion.11 = f32[4,512]{1,0:T(4,128)S(1)} fusion(bf16[4,1024]{1,0:T(4,128)(2,1)S(1)} %convert_element_type.30, bf16[512,1024]{1,0:T(8,128)(2,1)S(1)} %copy-done.1), kind=kOutput, calls=%fused_computation.33 | convolution fusion | flops 4194304 | bytes 1064960 | tf_op jit(solution)/shard_map/ep,qp->eq/dot_general | solution.py:59
  18.7 0.0 collective-permute-done.1
  18.8 1.2 %collective-permute-start.5 = (bf16[4,1024]{1,0:T(4,128)(2,1)S(1)}, bf16[4,1024]{1,0:T(4,128)(2,1)S(1)}, u32[]{:S(2)}, u32[]{:S(2)}) collective-permute-start(bf16[4,1024]{1,0:T(4,128)(2,1)S(1)} %convert_element_type.30), channel_id=1, source_target_pairs={{0,9},{1,12},{4,13},{5,0},{8,1},{9,4},{12,5},{13,8},{2,11},{3,14},... | collective-permute-start | bytes 24584 | tf_op jit(solution)/shard_map/ppermute | solution.py:16
  20.0 0.0 collective-permute-done.2
  20.0 1.4 %collective-permute-start.6 = (bf16[4,1024]{1,0:T(4,128)(2,1)S(1)}, bf16[4,1024]{1,0:T(4,128)(2,1)S(1)}, u32[]{:S(2)}, u32[]{:S(2)}) collective-permute-start(bf16[4,1024]{1,0:T(4,128)(2,1)S(1)} %convert_element_type.30), channel_id=1, source_target_pairs={{0,12},{1,13},{4,0},{5,1},{8,4},{9,5},{12,8},{13,9},{2,14},{3,15},... | collective-permute-start | bytes 24584 | tf_op jit(solution)/shard_map/ppermute | solution.py:16
  21.4 0.0 collective-permute-done.3
  21.5 1.5 %collective-permute-start.7 = (bf16[4,1024]{1,0:T(4,128)(2,1)S(1)}, bf16[4,1024]{1,0:T(4,128)(2,1)S(1)}, u32[]{:S(2)}, u32[]{:S(2)}) collective-permute-start(bf16[4,1024]{1,0:T(4,128)(2,1)S(1)} %convert_element_type.30), channel_id=1, source_target_pairs={{0,13},{1,0},{4,1},{5,4},{8,5},{9,8},{12,9},{13,12},{2,15},{3,2},{... | collective-permute-start | bytes 24584 | tf_op jit(solution)/shard_map/ppermute | solution.py:16
  23.0 0.0 collective-permute-done.5
  23.0 0.8 %collective-permute-done.6 = bf16[4,1024]{1,0:T(4,128)(2,1)S(1)} collective-permute-done((bf16[4,1024]{1,0:T(4,128)(2,1)S(1)}, bf16[4,1024]{1,0:T(4,128)(2,1)S(1)}, u32[]{:S(2)}, u32[]{:S(2)}) %collective-permute-start.6) | collective-permute-done | bytes 8224 | tf_op jit(solution)/shard_map/ppermute | solution.py:16
  23.8 0.5 %collective-permute-done.7 = bf16[4,1024]{1,0:T(4,128)(2,1)S(1)} collective-permute-done((bf16[4,1024]{1,0:T(4,128)(2,1)S(1)}, bf16[4,1024]{1,0:T(4,128)(2,1)S(1)}, u32[]{:S(2)}, u32[]{:S(2)}) %collective-permute-start.7) | collective-permute-done | bytes 8224 | tf_op jit(solution)/shard_map/ppermute | solution.py:16
  24.3 0.6 %gather_fusion = bf16[8,4,1024]{2,1,0:T(4,128)(2,1)S(1)} fusion(bf16[8,4,1024]{2,1,0:T(4,128)(2,1)S(1)} %constant_dynamic-update-slice_fusion, s32[1024]{0:T(1024)S(1)} %pad_clamp_fusion), kind=kCustom, calls=%fused_computation | custom fusion | bytes 131104 | tf_op jit(solution)/shard_map/jit(_take)/gather | solution.py:19
  24.9 0.7 %multiply_reduce_fusion = f32[]{:T(128)} fusion(bf16[8,4,1024]{2,1,0:T(4,128)(2,1)S(1)} %gather_fusion), kind=kLoop, calls=%fused_computation.3 | loop fusion | flops 98303 | bytes 65540 | tf_op jit(solution)/shard_map/reduce_sum | solution.py:56
  26.3 1.1 %convolution_multiply_fusion = f32[128,1024]{1,0:T(8,128)} fusion(bf16[32,1024]{1,0:T(8,128)(2,1)S(1)} %reshape.86, s32[]{:T(128)S(6)} %select_n.30), kind=kOutput, calls=%fused_computation.1 | convolution fusion | flops 8519680 | bytes 598020 | tf_op jit(solution)/shard_map/ek,el->kl/dot_general | solution.py:54
  27.3 0.0 collective-permute-done.8
  27.3 0.4 %broadcast_select_fusion.1 = (f32[4,512]{1,0:T(4,128)S(1)}, f32[4,512]{1,0:T(4,128)S(1)}) fusion(f32[4,512]{1,0:T(4,128)S(1)} %fusion.11, pred[]{:T(512)S(6)} %eq.5, bf16[4,1024]{1,0:T(4,128)(2,1)S(1)} %convert_element_type.30, bf16[512,1024]{1,0:T(8,128)(2,1)S(1)} %collective-permute-done.8), kind=kOutput, calls=%fused_computation.20 | convolution fusion | flops 4198400 | bytes 1081345 | tf_op jit(solution)/shard_map/ep,qp->eq/dot_general | solution.py:60
  27.7 0.6 %maximum_multiply_fusion = f32[4,1024]{1,0:T(4,128)} fusion(f32[4,512]{1,0:T(4,128)S(1)} %get-tuple-element.5, f32[4,512]{1,0:T(4,128)S(1)} %get-tuple-element.4, f32[]{:T(128)S(6)} %rsqrt.3), kind=kLoop, calls=%fused_computation.16 | loop fusion | flops 8192 | bytes 32772 | tf_op jit(solution)/shard_map/mul | solution.py:66
  (19 shorter events, 0.2 us)
Async XLA Ops:
  0.6 1.2 %copy-start = (bf16[256,2048]{1,0:T(8,128)(2,1)S(1)}, bf16[256,2048]{1,0:T(8,128)(2,1)}, u32[]{:S(2)}) copy-start(bf16[256,2048]{1,0:T(8,128)(2,1)} %param.7) | copy-start | bytes 3145732
  0.6 8.9 %copy-start.1 = (bf16[512,1024]{1,0:T(8,128)(2,1)S(1)}, bf16[512,1024]{1,0:T(8,128)(2,1)}, u32[]{:S(2)}) copy-start(bf16[512,1024]{1,0:T(8,128)(2,1)} %param.11) | copy-start | bytes 3145732
  1.9 7.7 %copy-start.2 = (s32[4]{0:T(128)S(1)}, s32[4]{0:T(128)}, u32[]{:S(2)}) copy-start(s32[4]{0:T(128)} %param.8) | copy-start | bytes 52
  6.5 5.2 %collective-permute-start = (f32[256,64]{0,1:T(8,128)S(1)}, f32[256,64]{0,1:T(8,128)S(1)}, u32[]{:S(2)}, u32[]{:S(2)}) collective-permute-start(f32[256,64]{0,1:T(8,128)S(1)} %pad_maximum_fusion), channel_id=1, source_target_pairs={{0,2},{2,0},{1,3},{3,1},{4,6},{6,4},{5,7},{7,5},{8,10},{10,8},{9,1... | collective-permute-start | bytes 196616 | tf_op jit(solution)/shard_map/ppermute | solution.py:25
  9.6 17.8 %collective-permute-start.8 = (bf16[512,1024]{1,0:T(8,128)(2,1)S(1)}, bf16[512,1024]{1,0:T(8,128)(2,1)S(1)}, u32[]{:S(2)}, u32[]{:S(2)}) collective-permute-start(bf16[512,1024]{1,0:T(8,128)(2,1)S(1)} %copy-done.1), channel_id=1, source_target_pairs={{0,1},{1,0},{2,3},{3,2},{4,5},{5,4},{6,7},{7,6},{8,9},{9,8},{10,11... | collective-permute-start | bytes 3145736 | tf_op jit(solution)/shard_map/ppermute | solution.py:41
  12.4 6.4 %collective-permute-start.1 = (bf16[4,1024]{1,0:T(4,128)(2,1)S(1)}, bf16[4,1024]{1,0:T(4,128)(2,1)S(1)}, u32[]{:S(2)}, u32[]{:S(2)}) collective-permute-start(bf16[4,1024]{1,0:T(4,128)(2,1)S(1)} %convert_element_type.30), channel_id=1, source_target_pairs={{0,1},{1,4},{4,5},{5,8},{8,9},{9,12},{12,13},{13,0},{2,3},{3,6},{6... | collective-permute-start | bytes 24584 | tf_op jit(solution)/shard_map/ppermute | solution.py:16
  12.4 7.6 %collective-permute-start.2 = (bf16[4,1024]{1,0:T(4,128)(2,1)S(1)}, bf16[4,1024]{1,0:T(4,128)(2,1)S(1)}, u32[]{:S(2)}, u32[]{:S(2)}) collective-permute-start(bf16[4,1024]{1,0:T(4,128)(2,1)S(1)} %convert_element_type.30), channel_id=1, source_target_pairs={{0,4},{1,5},{4,8},{5,9},{8,12},{9,13},{12,0},{13,1},{2,6},{3,7},{6... | collective-permute-start | bytes 24584 | tf_op jit(solution)/shard_map/ppermute | solution.py:16
  14.6 6.8 %collective-permute-start.3 = (bf16[4,1024]{1,0:T(4,128)(2,1)S(1)}, bf16[4,1024]{1,0:T(4,128)(2,1)S(1)}, u32[]{:S(2)}, u32[]{:S(2)}) collective-permute-start(bf16[4,1024]{1,0:T(4,128)(2,1)S(1)} %convert_element_type.30), channel_id=1, source_target_pairs={{0,5},{1,8},{4,9},{5,12},{8,13},{9,0},{12,1},{13,4},{2,7},{3,10},{... | collective-permute-start | bytes 24584 | tf_op jit(solution)/shard_map/ppermute | solution.py:16
  17.1 5.8 %collective-permute-start.4 = (bf16[4,1024]{1,0:T(4,128)(2,1)S(1)}, bf16[4,1024]{1,0:T(4,128)(2,1)S(1)}, u32[]{:S(2)}, u32[]{:S(2)}) collective-permute-start(bf16[4,1024]{1,0:T(4,128)(2,1)S(1)} %convert_element_type.30), channel_id=1, source_target_pairs={{0,8},{1,9},{4,12},{5,13},{8,0},{9,1},{12,4},{13,5},{2,10},{3,11},... | collective-permute-start | bytes 24584 | tf_op jit(solution)/shard_map/ppermute | solution.py:16
  18.8 4.2 %collective-permute-start.5 = (bf16[4,1024]{1,0:T(4,128)(2,1)S(1)}, bf16[4,1024]{1,0:T(4,128)(2,1)S(1)}, u32[]{:S(2)}, u32[]{:S(2)}) collective-permute-start(bf16[4,1024]{1,0:T(4,128)(2,1)S(1)} %convert_element_type.30), channel_id=1, source_target_pairs={{0,9},{1,12},{4,13},{5,0},{8,1},{9,4},{12,5},{13,8},{2,11},{3,14},... | collective-permute-start | bytes 24584 | tf_op jit(solution)/shard_map/ppermute | solution.py:16
  20.0 3.7 %collective-permute-start.6 = (bf16[4,1024]{1,0:T(4,128)(2,1)S(1)}, bf16[4,1024]{1,0:T(4,128)(2,1)S(1)}, u32[]{:S(2)}, u32[]{:S(2)}) collective-permute-start(bf16[4,1024]{1,0:T(4,128)(2,1)S(1)} %convert_element_type.30), channel_id=1, source_target_pairs={{0,12},{1,13},{4,0},{5,1},{8,4},{9,5},{12,8},{13,9},{2,14},{3,15},... | collective-permute-start | bytes 24584 | tf_op jit(solution)/shard_map/ppermute | solution.py:16
  21.5 2.8 %collective-permute-start.7 = (bf16[4,1024]{1,0:T(4,128)(2,1)S(1)}, bf16[4,1024]{1,0:T(4,128)(2,1)S(1)}, u32[]{:S(2)}, u32[]{:S(2)}) collective-permute-start(bf16[4,1024]{1,0:T(4,128)(2,1)S(1)} %convert_element_type.30), channel_id=1, source_target_pairs={{0,13},{1,0},{4,1},{5,4},{8,5},{9,8},{12,9},{13,12},{2,15},{3,2},{... | collective-permute-start | bytes 24584 | tf_op jit(solution)/shard_map/ppermute | solution.py:16

commit v2 on v1

--- a/solution.py
+++ b/solution.py
@@ -10,13 +10,7 @@
     n = lax.axis_size(axes)
     if n > 8:
         return lax.all_gather(block, axes)
-    me = lax.axis_index(axes)
-    got = [block]
-    for step in range(1, n):
-        got.append(lax.ppermute(block, axes, [(i, (i + step) % n) for i in range(n)]))
-    stacked = jnp.stack(got)
-    order = (me - jnp.arange(n)) % n
-    return jnp.take(stacked, order, axis=0, mode="clip")
+    return lax.all_to_all(jnp.broadcast_to(block, (n, *block.shape)), axes, 0, 0)
 
 
 def sum_over(part, axis):

time: 28.8 us -> 26 us (0.903)
  starting transfers between devices: 13.1 us -> 8.41 us
  waiting for transfers between devices: 3.45 us -> 7.71 us
  local copies, waits for them, and re-layouts: 2.27 us -> 0.93 us
  matrix products: 6.66 us -> 5.89 us
    ppermute x7 -> x0, starting transfers between devices: 10.1 us -> none  [gather_all(): lax.ppermute(block, axes, [(i, (i + step) % n) for i in range(n)])]
    all_to_all x0 -> x1, waiting for transfers between devices: none -> 5.55 us  [gather_all(): lax.all_to_all(jnp.broadcast_to(block, (n, *block.shape)), axes, 0, 0)]
    all_to_all x0 -> x1, starting transfers between devices: none -> 5.41 us  [gather_all(): lax.all_to_all(jnp.broadcast_to(block, (n, *block.shape)), axes, 0, 0)]
    ppermute x7 -> x0, waiting for transfers between devices: 1.31 us -> none  [gather_all(): lax.ppermute(block, axes, [(i, (i + step) % n) for i in range(n)])]
    unnamed x13 -> x8, local copies, waits for them, and re-layouts: 1.3 us -> 0.02 us
    dot_general x1, matrix products: 1.32 us -> 0.41 us  [per_device(): part_out = jnp.dot(out_grad, proj_out, preferred_element_type=jnp.float32)]
    broadcast_in_dim x0 -> x1, local copies, waits for them, and re-layouts: none -> 0.65 us  [gather_all(): jnp.broadcast_to(block, (n, *block.shape))]
    gather x1 -> x0, local copies, waits for them, and re-layouts: 0.61 us -> none  [gather_all(): return jnp.take(stacked, order, axis=0, mode='clip')]
  transfers between devices with their start and end apart: 9 -> 3, of which waited for: 3 -> 2; matrix products, arithmetic and copies ran while one was open for 12% -> 13% of each run, Pallas kernels for 0% -> 0%
where the time goes in v2:
time: 26 us; the launch traced here: 25.7 us
  starting transfers between devices  8.41 us (32%)
  waiting for transfers between devices  7.71 us (30%)
  matrix products  5.89 us (23%)
  between operations  1.43 us (6%)
  other arithmetic  1.37 us (5%)
  local copies, waits for them, and re-layouts  0.93 us (4%)
    all_to_all x1, waiting for transfers between devices, gather_all(): lax.all_to_all(jnp.broadcast_to(block, (n, *block.shape)), axes, 0, 0)  5.55 us
    all_to_all x1, starting transfers between devices, gather_all(): lax.all_to_all(jnp.broadcast_to(block, (n, *block.shape)), axes, 0, 0)  5.41 us
    dot_general x1, matrix products, per_device(): part_in = jnp.dot(hidden, proj_in, preferred_element_type=jnp.float32)  3.46 us
    ppermute x1, starting transfers between devices, sum_over(): return part + lax.ppermute(part, axis, [(0, 1), (1, 0)])  3 us
    ppermute x1, waiting for transfers between devices, sum_over(): return part + lax.ppermute(part, axis, [(0, 1), (1, 0)])  2.16 us
    dot_general x1, matrix products, per_device(): jnp.einsum('ek,el->kl', mine, every, preferred_element_type=jnp.float32)  1.05 us
    broadcast_in_dim x1, local copies, waits for them, and re-layouts, gather_all(): jnp.broadcast_to(block, (n, *block.shape))  0.65 us
    reduce_sum x1, other arithmetic, per_device(): total = jnp.sum(wide * wide)  0.64 us
  transfers between devices with their start and end apart: 3, of which 2 were waited for; matrix products, arithmetic and copies ran while one was open for 13% of the time, Pallas kernels for 0%

profile of v2, /device:TPU:0, one launch (start us, length us, event | category | flops | bytes accessed | tf_op | source)
XLA Modules:
  0.0 25.7 jit_solution(9764162142833299429)
XLA Ops:
  0.6 0.0 copy-start
  0.6 0.0 copy-start.2
  0.7 0.0 copy-start.1
  0.7 0.0 copy-start.3
  0.7 3.5 %fusion.7 = f32[256,32]{0,1:T(8,128)S(1)} fusion(bf16[256,7168]{1,0:T(8,128)(2,1)} %param.6, bf16[7168,32]{0,1:T(8,128)(2,1)} %param.9), kind=kOutput, calls=%fused_computation.16 | convolution fusion | flops 117440512 | bytes 4161536 | tf_op jit(solution)/shard_map/dot_general | solution.py:36
  4.1 0.0 copy-done
  4.2 0.0 copy-done.2
  4.2 0.4 %fusion.8 = f32[256,32]{0,1:T(8,128)S(1)} fusion(bf16[256,2048]{1,0:T(8,128)(2,1)S(1)} %copy-done, bf16[2048,32]{0,1:T(8,128)(2,1)S(1)} %copy-done.2), kind=kOutput, calls=%fused_computation.17 | convolution fusion | flops 33554432 | bytes 1212416 | tf_op jit(solution)/shard_map/dot_general | solution.py:37
  4.6 3.0 %collective-permute-start = (f32[256,64]{0,1:T(8,128)S(1)}, f32[256,64]{0,1:T(8,128)S(1)}, u32[]{:S(2)}, u32[]{:S(2)}) collective-permute-start(f32[256,64]{0,1:T(8,128)S(1)} %pad_maximum_fusion), channel_id=1, source_target_pairs={{0,2},{2,0},{1,3},{3,1},{4,6},{6,4},{5,7},{7,5},{8,10},{10,8},{9,1... | collective-permute-start | bytes 196616 | tf_op jit(solution)/shard_map/ppermute | solution.py:19
  7.6 0.0 copy-done.1
  7.6 0.0 collective-permute-start.1
  7.6 0.0 copy-done.3
  7.6 0.1 fusion.3
  7.7 2.2 %collective-permute-done = f32[256,64]{0,1:T(8,128)S(1)} collective-permute-done((f32[256,64]{0,1:T(8,128)S(1)}, f32[256,64]{0,1:T(8,128)S(1)}, u32[]{:S(2)}, u32[]{:S(2)}) %collective-permute-start) | collective-permute-done | bytes 65568 | tf_op jit(solution)/shard_map/ppermute | solution.py:19
  9.9 0.1 reshape.34
  10.0 0.2 convolution_convert_fusion
  10.2 0.1 convert_element_type.19
  10.3 0.7 %broadcast_in_dim.2 = bf16[8,4,1024]{2,1,0:T(4,128)(2,1)} broadcast(bf16[4,1024]{1,0:T(4,128)(2,1)S(1)} %convert_element_type.19), dimensions={1,2} | broadcast | bytes 73728 | tf_op jit(solution)/shard_map/broadcast_in_dim | solution.py:13
  11.0 5.4 %all-to-all-start = ((bf16[8,4,1024]{2,1,0:T(4,128)(2,1)}), bf16[8,4,1024]{2,1,0:T(4,128)(2,1)S(1)}, u32[]{:S(2)}, u32[]{:S(2)}) async-start(bf16[8,4,1024]{2,1,0:T(4,128)(2,1)} %broadcast_in_dim.2), calls=%async_computation | async-start | bytes 131072 | tf_op jit(solution)/shard_map/all_to_all | solution.py:13
  16.4 0.4 %fusion.9 = f32[4,512]{1,0:T(4,128)S(1)} fusion(bf16[4,1024]{1,0:T(4,128)(2,1)S(1)} %convert_element_type.19, bf16[512,1024]{1,0:T(8,128)(2,1)S(1)} %copy-done.1), kind=kOutput, calls=%fused_computation.18 | convolution fusion | flops 4194304 | bytes 1064960 | tf_op jit(solution)/shard_map/ep,qp->eq/dot_general | solution.py:53
  16.8 5.5 %all-to-all-done = bf16[8,4,1024]{2,1,0:T(4,128)(2,1)S(1)} async-done(((bf16[8,4,1024]{2,1,0:T(4,128)(2,1)}), bf16[8,4,1024]{2,1,0:T(4,128)(2,1)S(1)}, u32[]{:S(2)}, u32[]{:S(2)}) %all-to-all-start) | async-done | bytes 65568 | tf_op jit(solution)/shard_map/all_to_all | solution.py:13
  22.3 0.6 %multiply_reduce_fusion = f32[]{:T(128)} fusion(bf16[8,4,1024]{2,1,0:T(4,128)(2,1)S(1)} %all-to-all-done), kind=kLoop, calls=%fused_computation.2 | loop fusion | flops 98303 | bytes 65540 | tf_op jit(solution)/shard_map/reduce_sum | solution.py:50
  23.7 1.1 %convolution_multiply_fusion = f32[128,1024]{1,0:T(8,128)} fusion(bf16[32,1024]{1,0:T(8,128)(2,1)S(1)} %reshape.35, s32[]{:T(128)S(6)} %select_n.15), kind=kOutput, calls=%fused_computation | convolution fusion | flops 8519680 | bytes 598020 | tf_op jit(solution)/shard_map/ek,el->kl/dot_general | solution.py:48
  24.7 0.0 collective-permute-done.1
  24.7 0.4 %broadcast_select_fusion.1 = (f32[4,512]{1,0:T(4,128)S(1)}, f32[4,512]{1,0:T(4,128)S(1)}) fusion(f32[4,512]{1,0:T(4,128)S(1)} %fusion.9, pred[]{:T(512)S(6)} %eq.3, bf16[4,1024]{1,0:T(4,128)(2,1)S(1)} %convert_element_type.19, bf16[512,1024]{1,0:T(8,128)(2,1)S(1)} %collective-permute-done.1), kind=kOutput, calls=%fused_computation.10 | convolution fusion | flops 4198400 | bytes 1081345 | tf_op jit(solution)/shard_map/ep,qp->eq/dot_general | solution.py:54
  25.1 0.6 %maximum_multiply_fusion = f32[4,1024]{1,0:T(4,128)} fusion(f32[4,512]{1,0:T(4,128)S(1)} %get-tuple-element.5, f32[4,512]{1,0:T(4,128)S(1)} %get-tuple-element.4, f32[]{:T(128)S(6)} %rsqrt.3), kind=kLoop, calls=%fused_computation.7 | loop fusion | flops 8192 | bytes 32772 | tf_op jit(solution)/shard_map/mul | solution.py:60
  (4 shorter events, 0.1 us)
Async XLA Ops:
  0.6 3.5 %copy-start = (bf16[256,2048]{1,0:T(8,128)(2,1)S(1)}, bf16[256,2048]{1,0:T(8,128)(2,1)}, u32[]{:S(2)}) copy-start(bf16[256,2048]{1,0:T(8,128)(2,1)} %param.7) | copy-start | bytes 3145732
  0.6 3.5 %copy-start.2 = (bf16[2048,32]{0,1:T(8,128)(2,1)S(1)}, bf16[2048,32]{0,1:T(8,128)(2,1)}, u32[]{:S(2)}) copy-start(bf16[2048,32]{0,1:T(8,128)(2,1)} %param.10) | copy-start | bytes 393220
  0.7 7.0 %copy-start.1 = (bf16[512,1024]{1,0:T(8,128)(2,1)S(1)}, bf16[512,1024]{1,0:T(8,128)(2,1)}, u32[]{:S(2)}) copy-start(bf16[512,1024]{1,0:T(8,128)(2,1)} %param.11) | copy-start | bytes 3145732
  0.7 7.0 %copy-start.3 = (s32[4]{0:T(128)S(1)}, s32[4]{0:T(128)}, u32[]{:S(2)}) copy-start(s32[4]{0:T(128)} %param.8) | copy-start | bytes 52
  4.6 5.2 %collective-permute-start = (f32[256,64]{0,1:T(8,128)S(1)}, f32[256,64]{0,1:T(8,128)S(1)}, u32[]{:S(2)}, u32[]{:S(2)}) collective-permute-start(f32[256,64]{0,1:T(8,128)S(1)} %pad_maximum_fusion), channel_id=1, source_target_pairs={{0,2},{2,0},{1,3},{3,1},{4,6},{6,4},{5,7},{7,5},{8,10},{10,8},{9,1... | collective-permute-start | bytes 196616 | tf_op jit(solution)/shard_map/ppermute | solution.py:19
  7.6 17.1 %collective-permute-start.1 = (bf16[512,1024]{1,0:T(8,128)(2,1)S(1)}, bf16[512,1024]{1,0:T(8,128)(2,1)S(1)}, u32[]{:S(2)}, u32[]{:S(2)}) collective-permute-start(bf16[512,1024]{1,0:T(8,128)(2,1)S(1)} %copy-done.1), channel_id=1, source_target_pairs={{0,1},{1,0},{2,3},{3,2},{4,5},{5,4},{6,7},{7,6},{8,9},{9,8},{10,11... | collective-permute-start | bytes 3145736 | tf_op jit(solution)/shard_map/ppermute | solution.py:35
  11.0 11.3 %all-to-all-start = ((bf16[8,4,1024]{2,1,0:T(4,128)(2,1)}), bf16[8,4,1024]{2,1,0:T(4,128)(2,1)S(1)}, u32[]{:S(2)}, u32[]{:S(2)}) async-start(bf16[8,4,1024]{2,1,0:T(4,128)(2,1)} %broadcast_in_dim.2), calls=%async_computation | async-start | bytes 131072 | tf_op jit(solution)/shard_map/all_to_all | solution.py:13
